TPU v7x, 32 devices: a whole 2x2x4 slice. The times are simulated.
32 devices in a mesh: ma: 16 (over z, x, core), bl: 2 (over y).
Axes of the slice: x: 2, y: 2, z: 4, core: 2. Of those that a mesh axis runs over, the one named last changes fastest.
Arguments:
- visibilities: bfloat16 [2, 4160, 8192], P(None, 'bl', 'ma'), may hold values from -6 to 6
- beam_blocks: bfloat16 [16, 2, 4160, 1000], P('ma', None, 'bl'), may hold values from -0.125 to 0.125
- feed_pairs: int32 [4160, 2], P('bl'), may hold values from 0 to 1023
- feed_gains: float32 [2, 1024], replicated, may hold values from -1.5 to 1.5
- m_order: int32 [16], replicated, may hold values from 0 to 15, each once
Outputs:
- sky_modes: float32 [2, 16, 1000], P(None, 'ma', 'bl')
All inputs are finite; a program needn't handle non-finite values.
Results may differ from a plain program's by a relative error of at most 0.0049.
Values may be sent and summed in bfloat16 or wider, within the bound.
A program may use at most 64 MiB of HBM per device.

v0:
```python
import functools

import jax
import jax.numpy as jnp
import numpy as np
from jax import lax
from jax.experimental import pallas as pl
from jax.experimental.pallas import tpu as pltpu
from jax.sharding import PartitionSpec as P

NT = 8192
LANES = 128
CHUNKS = 2
PIECE = 1024
VMEM_LIMIT = 55216 * 2**10
MESH = pl.DeviceIdType.MESH


def trig(k):
    quarter = NT // 4
    turn = (k + quarter // 2) // quarter
    x = (k - turn * quarter).astype(jnp.float32) * np.float32(2.0 * np.pi / NT)
    y = x * x
    sin_x = x * (1.0 + y * (-1.0 / 6 + y * (1.0 / 120 + y * (-1.0 / 5040 + y * (1.0 / 362880)))))
    cos_x = 1.0 + y * (-0.5 + y * (1.0 / 24 + y * (-1.0 / 720 + y * (1.0 / 40320))))
    odd = (turn & 1) == 1
    cos_k = jnp.where(odd, sin_x, cos_x)
    sin_k = jnp.where(odd, cos_x, sin_x)
    cos_k = jnp.where(((turn + 1) & 2) == 2, -cos_k, cos_k)
    sin_k = jnp.where((turn & 2) == 2, -sin_k, sin_k)
    return cos_k, sin_k


def kernel(
    n_ma, n_bl, vis, beam, pairs, gains, order, out,
    vis_v, beam_v, pairs_v, gains_v, order_s,
    sums, near, part, got, rem_sums, rem_near, rem_part, rem_got, table, factor, lhs, share,
    vis_sem, beam_sem, small_sem, near_send, near_recv, send_sem, recv_sem, bl_send, bl_recv,
):
    me = lax.axis_index("ma")
    my_bl = lax.axis_index("bl")
    rows = vis.shape[1]
    local_times = vis.shape[2]
    cols = rows // LANES
    rem = rows - cols * LANES
    per = cols // CHUNKS
    chips = n_ma // 2
    chip = me // 2
    core = lax.rem(me, 2)
    other = 1 - core
    sibling = chip * 2 + other
    far = [lax.rem(chip + k, chips) for k in range(chips)]
    far_order = sorted(range(1, chips), key=lambda k: abs(k - chips // 2))

    order_copy = pltpu.make_async_copy(order, order_s, small_sem.at[0])
    order_copy.start()
    spans = [(c * per * LANES, per * LANES) for c in range(CHUNKS)] + [(cols * LANES, rem)]
    load_order = [0, CHUNKS] + list(range(1, CHUNKS))
    pieces = {}
    for c in load_order:
        start, size = spans[c]
        pieces[c] = [(at, min(PIECE, start + size - at)) for at in range(start, start + size, PIECE)]
    vis_copies, beam_copies = {}, {}
    slot = 0
    for c in load_order:
        for at, size in pieces[c]:
            for p in range(2):
                piece = pl.ds(at, size)
                vis_copies[at, p] = pltpu.make_async_copy(vis.at[p, piece], vis_v.at[p, piece], vis_sem.at[slot])
                vis_copies[at, p].start()
                beam_copies[at, p] = pltpu.make_async_copy(
                    beam.at[0, p, piece], beam_v.at[p, piece], beam_sem.at[slot]
                )
                slot += 1
    pairs_copy = pltpu.make_async_copy(pairs, pairs_v, small_sem.at[1])
    pairs_copy.start()
    gains_copy = pltpu.make_async_copy(gains, gains_v, small_sem.at[2])
    gains_copy.start()

    barrier = pltpu.get_barrier_semaphore()
    pl.semaphore_signal(barrier, inc=1, device_id={"ma": sibling}, device_id_type=MESH)
    for k in range(1, chips):
        pl.semaphore_signal(barrier, inc=1, device_id={"ma": far[k] * 2 + core}, device_id_type=MESH)
    bl_peers = [lax.rem(my_bl + k, n_bl) for k in range(n_bl)]
    for k in range(1, n_bl):
        pl.semaphore_signal(barrier, inc=1, device_id={"bl": bl_peers[k]}, device_id_type=MESH)

    order_copy.wait()
    row_of = lax.broadcasted_iota(jnp.int32, (n_ma, LANES), 0)
    m_value = jnp.zeros((n_ma, LANES), jnp.int32)
    for j in range(n_ma):
        m_value = jnp.where(row_of == (j % 2) * chips + j // 2, order_s[j] - n_ma // 2, m_value)
    left, right = [], []
    for block in range(local_times // LANES):
        time = me * local_times + block * LANES + lax.broadcasted_iota(jnp.int32, (n_ma, LANES), 1)
        cos_k, sin_k = trig((time * m_value) & (NT - 1))
        scale = np.float32(1.0 / np.sqrt(np.float32(NT)))
        cos_k, sin_k = cos_k * scale, sin_k * scale
        left.append(jnp.concatenate([cos_k, -sin_k], axis=0).T.astype(jnp.bfloat16))
        right.append(jnp.concatenate([sin_k, cos_k], axis=0).T.astype(jnp.bfloat16))
    left = jnp.concatenate(left, axis=0)
    right = jnp.concatenate(right, axis=0)

    def transform(start, size):
        flat = jnp.dot(vis_v[0, start:start + size, :], left, preferred_element_type=jnp.float32)
        flat = flat + jnp.dot(vis_v[1, start:start + size, :], right, preferred_element_type=jnp.float32)
        return flat.T

    near_copies = {}

    def to_sibling(c, source, target):
        near_copies[c] = pltpu.make_async_remote_copy(
            src_ref=source, dst_ref=target, send_sem=near_send.at[c], recv_sem=near_recv.at[c],
            device_id={"ma": sibling}, device_id_type=MESH,
        )
        near_copies[c].start()

    def start_beam(which):
        for c in which:
            for at, _ in pieces[c]:
                for p in range(2):
                    beam_copies[at, p].start()

    far_copies = {}

    def to_far(c):
        near_copies[c].wait_recv()
        if c == CHUNKS:
            rem_part[...] = rem_sums[core] + rem_near[...]
        else:
            both = sums[c, core] + near[c]
            sums[c, core] = both
            part[c] = both.astype(jnp.bfloat16).reshape(chips, 2 * per, LANES)
        for k in far_order:
            source = rem_part.at[far[k]] if c == CHUNKS else part.at[c, far[k]]
            target = rem_got.at[chip] if c == CHUNKS else got.at[c, chip]
            far_copies[c, k] = pltpu.make_async_remote_copy(
                src_ref=source, dst_ref=target, send_sem=send_sem.at[c, k], recv_sem=recv_sem.at[c, k],
                device_id={"ma": far[k] * 2 + core}, device_id_type=MESH,
            )
            far_copies[c, k].start()

    for c in load_order:
        for number, (at, size) in enumerate(pieces[c]):
            for p in range(2):
                vis_copies[at, p].wait()
            if c == load_order[-1] and number == 0:
                start_beam(load_order[:-1])
            if c == CHUNKS:
                flat = transform(at, size)
                wide = jnp.concatenate(
                    [flat[:n_ma], flat[n_ma:], jnp.zeros((n_ma, LANES - 2 * rem), jnp.float32)], axis=1
                )
                for j in range(n_ma):
                    rem_sums[j // chips, j % chips] = wide[j:j + 1, :]
                continue
            for begin in range(at, at + size, 2 * LANES):
                flat = transform(begin, 2 * LANES)
                for u in range(2):
                    row = (begin - spans[c][0]) // LANES + u
                    for p in range(2):
                        for g in range(2):
                            from_row = p * n_ma + g * chips
                            sums[c, g, pl.ds(p * per + row, chips, stride=2 * per), :] = (
                                flat[from_row:from_row + chips, u * LANES:(u + 1) * LANES]
                            )
        if c == 0:
            pl.semaphore_wait(barrier, 1 + chips - 1 + n_bl - 1)
        if c == CHUNKS:
            to_sibling(c, rem_sums.at[other], rem_near)
        else:
            to_sibling(c, sums.at[c, other], near.at[c])

    for c in load_order[:-1]:
        to_far(c)
    start_beam(load_order[-1:])

    pairs_copy.wait()
    gains_copy.wait()
    high = gains.shape[1] // LANES
    for comp in range(2):
        for h in range(high):
            table[comp * high + h:comp * high + h + 1, :] = gains_v[comp:comp + 1, h * LANES:(h + 1) * LANES]
    whole = table[...]
    first = whole.astype(jnp.bfloat16)
    rest = whole - first.astype(jnp.float32)
    second = rest.astype(jnp.bfloat16)
    third = (rest - second.astype(jnp.float32)).astype(jnp.bfloat16)
    thirds = jnp.concatenate([first, second, third], axis=0)

    def gain_of(feed, start, size):
        index = pairs_v[feed:feed + 1, start:start + size]
        low = lax.broadcasted_iota(jnp.int32, (LANES, size), 0)
        hot = jnp.where(low == (index & (LANES - 1)), 1.0, 0.0).astype(jnp.bfloat16)
        picked = jnp.dot(thirds, hot, preferred_element_type=jnp.float32)
        picked = picked[:2 * high] + picked[2 * high:4 * high] + picked[4 * high:]
        mask = lax.broadcasted_iota(jnp.int32, (high, size), 0) == index // LANES
        re = jnp.sum(jnp.where(mask, picked[:high], 0.0), axis=0, keepdims=True)
        im = jnp.sum(jnp.where(mask, picked[high:], 0.0), axis=0, keepdims=True)
        return re, im

    def factor_of(start, size):
        a_re, a_im = gain_of(0, start, size)
        b_re, b_im = gain_of(1, start, size)
        return a_re * b_re + a_im * b_im, a_im * b_re - a_re * b_im

    for i in range(0, cols, 2):
        f_re, f_im = factor_of(i * LANES, 2 * LANES)
        for u in range(2):
            factor[0, i + u:i + u + 1, :] = f_re[:, u * LANES:(u + 1) * LANES]
            factor[1, i + u:i + u + 1, :] = f_im[:, u * LANES:(u + 1) * LANES]
    rem_re, rem_im = factor_of(*spans[CHUNKS])

    to_far(load_order[-1])

    def weigh(s_re, s_im, f_re, f_im):
        s_re = s_re.astype(jnp.bfloat16).astype(jnp.float32)
        s_im = s_im.astype(jnp.bfloat16).astype(jnp.float32)
        return s_re * f_re - s_im * f_im, s_re * f_im + s_im * f_re

    total = None
    for c in load_order:
        for k in far_order:
            far_copies[c, k].wait_recv()
        start, size = spans[c]
        at = slice(start, start + size)
        if c == CHUNKS:
            tail = rem_part[chip]
            for k in far_order:
                tail = tail + rem_got[far[k]]
            w_re, w_im = weigh(tail[:, :rem], tail[:, rem:2 * rem], rem_re, rem_im)
            lhs[0:1, at] = w_re
            lhs[1:2, at] = w_im
        else:
            mine = pl.multiple_of(chip * 2 * per, 2 * per)
            spectra = sums[c, core, pl.ds(mine, 2 * per), :]
            for k in far_order:
                spectra = spectra + got[c, far[k]].astype(jnp.float32)
            w_re, w_im = weigh(
                spectra[:per], spectra[per:], factor[0, c * per:(c + 1) * per], factor[1, c * per:(c + 1) * per]
            )
            for i in range(per):
                lane = slice(start + i * LANES, start + (i + 1) * LANES)
                lhs[0:1, lane] = w_re[i:i + 1]
                lhs[1:2, lane] = w_im[i:i + 1]
        for begin, size in pieces[c]:
            at = slice(begin, begin + size)
            w_re, w_im = lhs[0:1, at], lhs[1:2, at]
            rows_of = [
                jnp.concatenate([w_re, w_im], axis=0).astype(jnp.bfloat16),
                jnp.concatenate([w_im, -w_re], axis=0).astype(jnp.bfloat16),
            ]
            for p in range(2):
                beam_copies[begin, p].wait()
                term = jnp.dot(rows_of[p], beam_v[p, at, :], preferred_element_type=jnp.float32)
                total = term if total is None else total + term

    width = beam.shape[3] // n_bl
    for d in range(n_bl):
        share[d, :, 0, 0:width] = total[:, d * width:(d + 1) * width]
    bl_copies = []
    for k in range(1, n_bl):
        copy = pltpu.make_async_remote_copy(
            src_ref=share.at[bl_peers[k]], dst_ref=out.at[my_bl],
            send_sem=bl_send.at[k], recv_sem=bl_recv.at[k],
            device_id={"bl": bl_peers[k]}, device_id_type=MESH,
        )
        copy.start()
        bl_copies.append(copy)
    out[my_bl] = share[my_bl]
    for copy in near_copies.values():
        copy.wait_send()
    for copy in far_copies.values():
        copy.wait_send()
    for copy in bl_copies:
        copy.wait_send()
    for copy in bl_copies:
        copy.wait_recv()


def per_device(n_ma, n_bl, visibilities, beam_blocks, feed_pairs, feed_gains, m_order):
    _, rows, local_times = visibilities.shape
    width = beam_blocks.shape[3]
    assert m_order.shape[0] == n_ma and beam_blocks.shape[0] == 1 and n_ma % 16 == 0
    cols = rows // LANES
    rem = rows - cols * LANES
    per = cols // CHUNKS
    assert per * LANES % PIECE == 0 and cols % CHUNKS == 0 and (2 * per) % 16 == 0 and 0 < 2 * rem <= LANES
    chips = n_ma // 2
    share_width = width // n_bl
    share_pad = -(-share_width // LANES) * LANES
    feeds = feed_gains.shape[1]
    f32, bf16 = jnp.float32, jnp.bfloat16
    dma = pltpu.SemaphoreType.DMA
    parts = pl.pallas_call(
        functools.partial(kernel, n_ma, n_bl),
        out_shape=jax.ShapeDtypeStruct((n_bl, 2, 1, share_pad), f32),
        in_specs=[pl.BlockSpec(memory_space=pl.ANY)] * 5,
        out_specs=pl.BlockSpec(memory_space=pltpu.VMEM),
        scratch_shapes=[
            pltpu.VMEM((2, rows, local_times), bf16),
            pltpu.VMEM((2, rows, width), bf16),
            pltpu.VMEM((2, rows), jnp.int32),
            pltpu.VMEM((2, feeds), f32),
            pltpu.SMEM((n_ma,), jnp.int32),
            pltpu.VMEM((CHUNKS, 2, chips * 2 * per, LANES), f32),
            pltpu.VMEM((CHUNKS, chips * 2 * per, LANES), f32),
            pltpu.VMEM((CHUNKS, chips, 2 * per, LANES), bf16),
            pltpu.VMEM((CHUNKS, chips, 2 * per, LANES), bf16),
            pltpu.VMEM((2, chips, 1, LANES), f32),
            pltpu.VMEM((chips, 1, LANES), f32),
            pltpu.VMEM((chips, 1, LANES), f32),
            pltpu.VMEM((chips, 1, LANES), f32),
            pltpu.VMEM((2 * feeds // LANES, LANES), f32),
            pltpu.VMEM((2, cols, LANES), f32),
            pltpu.VMEM((8, rows), f32),
            pltpu.VMEM((n_bl, 2, 1, share_pad), f32),
            dma((2 * (cols * LANES // PIECE + 1),)),
            dma((2 * (cols * LANES // PIECE + 1),)),
            dma((3,)),
            dma((CHUNKS + 1,)),
            dma((CHUNKS + 1,)),
            dma((CHUNKS + 1, chips)),
            dma((CHUNKS + 1, chips)),
            dma((n_bl,)),
            dma((n_bl,)),
        ],
        compiler_params=pltpu.CompilerParams(
            collective_id=0, has_side_effects=True, vmem_limit_bytes=VMEM_LIMIT
        ),
        cost_estimate=pl.CostEstimate(
            flops=2 * rows * (2 * local_times * 2 * n_ma + 4 * width),
            bytes_accessed=4 * rows * (local_times + width),
            transcendentals=0,
        ),
    )(visibilities, beam_blocks, feed_pairs.T, feed_gains, m_order)
    result = parts[0, :, :, :share_width]
    for d in range(1, n_bl):
        result = result + parts[d, :, :, :share_width]
    return result


def solution(mesh):
    return jax.shard_map(
        functools.partial(per_device, mesh.shape["ma"], mesh.shape["bl"]),
        mesh=mesh,
        in_specs=(P(None, "bl", "ma"), P("ma", None, "bl", None), P("bl", None), P(), P()),
        out_specs=P(None, "ma", "bl"),
        check_vma=False,
    )
```

profile of v0, /device:TPU:0, one launch (start us, length us, event | category | flops | bytes accessed | tf_op | source)
XLA Modules:
  0.0 17.8 jit_solution(10855519125674013848)
XLA Ops:
  0.0 0.0 copy-start
  0.0 0.7 %copy-done = s32[16]{0:T(128)S(1)} copy-done((s32[16]{0:T(128)S(1)}, s32[16]{0:T(128)}, u32[]{:S(2)}) %copy-start) | copy-done | bytes 88
  0.7 16.6 %shard_map.55 = f32[2,2,1,512]{3,2,1,0:T(1,128)S(1)} custom-call(bf16[2,2080,512]{2,1,0:T(8,128)(2,1)} %vis.1, bf16[1,2,2080,1000]{3,2,1,0:T(8,128)(2,1)} %beam.1, s32[2,2080]{1,0:T(2,128)} %bitcast.3, f32[2,1024]{1,0:T(2,128)} %gains.1, s32[16]{0:T(128)S(1)} %copy-done), custom_call_target="tpu_custom_call" | custom-call | flops 152954880 | bytes 12579840 | tf_op jit(solution)/shard_map/pallas_call | solution.py:295
  17.2 0.6 %add_bitcast_fusion = f32[2,1,500]{2,1,0:T(1,128)} fusion(f32[2,2,1,512]{3,2,1,0:T(1,128)S(1)} %shard_map.55), kind=kLoop, calls=%fused_computation | loop fusion | flops 1000 | bytes 12000 | tf_op jit(solution)/shard_map/add | solution.py:339
Async XLA Ops:
  0.0 0.7 %copy-start = (s32[16]{0:T(128)S(1)}, s32[16]{0:T(128)}, u32[]{:S(2)}) copy-start(s32[16]{0:T(128)} %order.1) | copy-start | bytes 196
where the time goes:
time: 18 us; the launch traced here: 17.8 us
  Pallas kernels  16.6 us (92%)
  local copies, waits for them, and re-layouts  0.65 us (4%)
  other arithmetic  0.6 us (3%)
    pallas_call x1, Pallas kernels, per_device(): pl.pallas_call(functools.partial(kernel, n_ma, n_bl), out_shape=jax.Shape...  16.6 us
    unnamed x2, local copies, waits for them, and re-layouts  0.65 us
    add x1, other arithmetic, per_device(): result = result + parts[d, :, :, :share_width]  0.6 us

commit v1 on v0

--- a/solution.py
+++ b/solution.py
@@ -218,7 +218,12 @@
         s_im = s_im.astype(jnp.bfloat16).astype(jnp.float32)
         return s_re * f_re - s_im * f_im, s_re * f_im + s_im * f_re
 
-    total = None
+    full = beam.shape[3]
+    split = (full + 255) // 256 // 2 * 256
+    tail_total = jnp.zeros((2, full), jnp.float32)
+    low_total = jnp.zeros((2, split), jnp.float32)
+    high_re = jnp.zeros((16, full - split), jnp.float32)
+    high_im = jnp.zeros((16, full - split), jnp.float32)
     for c in load_order:
         for k in far_order:
             far_copies[c, k].wait_recv()
@@ -243,6 +248,7 @@
                 lane = slice(start + i * LANES, start + (i + 1) * LANES)
                 lhs[0:1, lane] = w_re[i:i + 1]
                 lhs[1:2, lane] = w_im[i:i + 1]
+        columns = [w.astype(jnp.bfloat16).astype(jnp.float32).T for w in (w_re, w_im)] if c < CHUNKS else None
         for begin, size in pieces[c]:
             at = slice(begin, begin + size)
             w_re, w_im = lhs[0:1, at], lhs[1:2, at]
@@ -252,9 +258,30 @@
             ]
             for p in range(2):
                 beam_copies[begin, p].wait()
-                term = jnp.dot(rows_of[p], beam_v[p, at, :], preferred_element_type=jnp.float32)
-                total = term if total is None else total + term
-
+            if c == CHUNKS:
+                for p in range(2):
+                    tail_total = tail_total + jnp.dot(
+                        rows_of[p], beam_v[p, at, :], preferred_element_type=jnp.float32
+                    )
+                continue
+            for p in range(2):
+                low_total = low_total + jnp.dot(
+                    rows_of[p], beam_v[p, at, :split], preferred_element_type=jnp.float32
+                )
+            for row in range(begin, begin + size, 16):
+                col = (row - start) // LANES
+                r = (row - start) % LANES
+                v_re = columns[0][r:r + 16, col:col + 1]
+                v_im = columns[1][r:r + 16, col:col + 1]
+                b_re = beam_v[0, row:row + 16, split:].astype(jnp.float32)
+                b_im = beam_v[1, row:row + 16, split:].astype(jnp.float32)
+                high_re = high_re + (b_re * v_re + b_im * v_im)
+                high_im = high_im + (b_re * v_im - b_im * v_re)
+
+    high = jnp.concatenate(
+        [jnp.sum(high_re, axis=0, keepdims=True), jnp.sum(high_im, axis=0, keepdims=True)], axis=0
+    )
+    total = tail_total + jnp.concatenate([low_total, high], axis=1)
     width = beam.shape[3] // n_bl
     for d in range(n_bl):
         share[d, :, 0, 0:width] = total[:, d * width:(d + 1) * width]

time: 18 us -> 18.6 us (1.033)
  Pallas kernels: 16.6 us -> 17.1 us
    pallas_call x1, Pallas kernels: 16.6 us -> 17.1 us  [per_device(): pl.pallas_call(functools.partial(kernel, n_ma, n_bl), out_shape=jax.Shape...]
where the time goes in v1:
time: 18.6 us; the launch traced here: 18.4 us
  Pallas kernels  17.1 us (92%)
  local copies, waits for them, and re-layouts  0.65 us (3%)
  other arithmetic  0.6 us (3%)
    pallas_call x1, Pallas kernels, per_device(): pl.pallas_call(functools.partial(kernel, n_ma, n_bl), out_shape=jax.Shape...  17.1 us
    unnamed x2, local copies, waits for them, and re-layouts  0.65 us
    add x1, other arithmetic, per_device(): result = result + parts[d, :, :, :share_width]  0.6 us

profile of v1, /device:TPU:0, one launch (start us, length us, event | category | flops | bytes accessed | tf_op | source)
XLA Modules:
  0.0 18.4 jit_solution(15583470597909297917)
XLA Ops:
  0.0 0.0 copy-start
  0.0 0.7 %copy-done = s32[16]{0:T(128)S(1)} copy-done((s32[16]{0:T(128)S(1)}, s32[16]{0:T(128)}, u32[]{:S(2)}) %copy-start) | copy-done | bytes 88
  0.7 17.1 %shard_map.55 = f32[2,2,1,512]{3,2,1,0:T(1,128)S(1)} custom-call(bf16[2,2080,512]{2,1,0:T(8,128)(2,1)} %vis.1, bf16[1,2,2080,1000]{3,2,1,0:T(8,128)(2,1)} %beam.1, s32[2,2080]{1,0:T(2,128)} %bitcast.3, f32[2,1024]{1,0:T(2,128)} %gains.1, s32[16]{0:T(128)S(1)} %copy-done), custom_call_target="tpu_custom_call" | custom-call | flops 152954880 | bytes 12579840 | tf_op jit(solution)/shard_map/pallas_call | solution.py:322
  17.8 0.6 %add_bitcast_fusion = f32[2,1,500]{2,1,0:T(1,128)} fusion(f32[2,2,1,512]{3,2,1,0:T(1,128)S(1)} %shard_map.55), kind=kLoop, calls=%fused_computation | loop fusion | flops 1000 | bytes 12000 | tf_op jit(solution)/shard_map/add | solution.py:366
Async XLA Ops:
  0.0 0.7 %copy-start = (s32[16]{0:T(128)S(1)}, s32[16]{0:T(128)}, u32[]{:S(2)}) copy-start(s32[16]{0:T(128)} %order.1) | copy-start | bytes 196
